TPU v7x, 32 devices: a whole 2x2x4 slice. The times are simulated.
32 devices in a mesh: groups: 2 (over y), wide: 16 (over z, x, core), narrow: 1.
Axes of the slice: x: 2, y: 2, z: 4, core: 2. Of those that a mesh axis runs over, the one named last changes fastest.
Arguments:
- tokens: bfloat16 [4096, 8192], P(('groups', 'wide'), 'narrow'), parts along dimension 0, may hold values from -6 to 6
- adapter_down_weight: bfloat16 [16, 2, 4096, 128], P(None, 'narrow', 'wide'), may hold values from -0.0625 to 0.0625
- adapter_up_weight: bfloat16 [16, 2, 512, 128], P(None, 'narrow', 'wide'), may hold values from -0.75 to 0.75
- adapter_entry: int32 [16], replicated, may hold values from 0 to 15, each once
- adapter_of_request: int32 [8], P('groups'), parts along dimension 0, may hold values from 0 to 15
- token_blocks_per_request: int32 [8], P('groups'), parts along dimension 0, may hold values from 1 to 8, 16 in all
Outputs:
- key_delta: bfloat16 [4096, 1024], P(('groups', 'wide'), 'narrow'), parts along dimension 0
- value_delta: bfloat16 [4096, 1024], P(('groups', 'wide'), 'narrow'), parts along dimension 0
There are 2 independent parts, one for each index of `groups`. A program takes and returns all parts, laid end to end along the dimension named above; an argument that names none is the same for every part. Nothing has to cross between parts.
Inputs may be any that keep to these rules, and one draw needn't show every extreme that they name: `adapter_entry`: each table entry holds exactly one adapter. `token_blocks_per_request`: the counts sum to 16.
All inputs are finite; a program needn't handle non-finite values.
Results may differ from a plain program's by a relative error of at most 0.0049.
Values may be sent and summed in bfloat16 or wider, within the bound.
No kernel may reach another device: no remote copies, remote signals or barrier semaphores. Data moves between devices by JAX's collectives and lax.ppermute only.
A program may use at most 64 MiB of HBM per device.

v0:
```python
import jax
import jax.numpy as jnp
from jax import lax
from jax.experimental import pallas as pl
from jax.experimental.pallas import tpu as pltpu
from jax.sharding import PartitionSpec as P

BLK = 128
PLANE = 4
SLOTS = 3
USUAL = 2


def block_tables(
    adapter_entry,
    adapter_of_request,
    token_blocks_per_request,
    block_count,
    request_count,
    adapter_count,
):
    request_ends = jnp.cumsum(token_blocks_per_request)
    block_index = jnp.arange(block_count, dtype=jnp.int32)
    request = jnp.sum((request_ends[None, :] <= block_index[:, None]).astype(jnp.int32), axis=1)
    pick_table = (request[:, None] == jnp.arange(request_count, dtype=jnp.int32)[None, :]).astype(
        jnp.int32
    )
    adapter = jnp.sum(pick_table * adapter_of_request[None, :], axis=1)
    slot_table = (adapter[:, None] == jnp.arange(adapter_count, dtype=jnp.int32)[None, :]).astype(
        jnp.int32
    )
    return jnp.sum(slot_table * adapter_entry[None, :], axis=1)


def direct_body(
    tokens,
    adapter_down_weight,
    adapter_up_weight,
    adapter_entry,
    adapter_of_request,
    token_blocks_per_request,
):
    wide_count = lax.axis_size("wide")
    blocks_dev = tokens.shape[0] // BLK
    local_width = tokens.shape[1]
    paired_ranks = adapter_down_weight.shape[3]
    rank_count = paired_ranks // 2
    slot_ids = block_tables(
        adapter_entry,
        adapter_of_request,
        token_blocks_per_request,
        blocks_dev * wide_count,
        token_blocks_per_request.shape[0],
        adapter_entry.shape[0],
    )
    needed_adapters = slot_ids.reshape(wide_count, blocks_dev).T
    down_outgoing = adapter_down_weight[needed_adapters]
    up_outgoing = adapter_up_weight[needed_adapters]
    got_down, got_up = (
        lax.all_to_all(down_outgoing, "wide", split_axis=1, concat_axis=3, tiled=True),
        lax.all_to_all(up_outgoing, "wide", split_axis=1, concat_axis=3, tiled=True),
    )
    got_down = got_down.reshape(blocks_dev, local_width, paired_ranks)
    block_rows = tokens.reshape(blocks_dev, BLK, local_width)
    shrink = jnp.einsum("btd,bdr->btr", block_rows, got_down, preferred_element_type=jnp.float32)
    low_rank = lax.psum(shrink, "narrow").astype(jnp.bfloat16)
    got_up = got_up.reshape(blocks_dev, -1, paired_ranks)
    delta_key = jnp.einsum(
        "btr,bjr->btj",
        low_rank[..., :rank_count],
        got_up[..., :rank_count],
        preferred_element_type=jnp.float32,
    )
    delta_value = jnp.einsum(
        "btr,bjr->btj",
        low_rank[..., rank_count:],
        got_up[..., rank_count:],
        preferred_element_type=jnp.float32,
    )
    out_cols = got_up.shape[1]
    key_delta = delta_key.reshape(blocks_dev * BLK, out_cols).astype(jnp.bfloat16)
    value_delta = delta_value.reshape(blocks_dev * BLK, out_cols).astype(jnp.bfloat16)
    return (key_delta, value_delta)


def swap(value, step):
    count = lax.axis_size("wide")
    return lax.ppermute(value, "wide", [(i, i ^ step) for i in range(count)])


def swap_cores(value):
    count = lax.axis_size("wide")
    pairs = [[i, i + 1] for i in range(0, count, 2)]
    return lax.all_to_all(value, "wide", 0, 0, axis_index_groups=pairs, tiled=True)


def pick(index, values):
    got = values[0]
    for i in range(1, len(values)):
        got = jnp.where(index == i, values[i], got)
    return got


def landed(out, sem):
    pltpu.make_async_copy(out, out, sem).wait()


def slices(tokens_ref, column, run, out, sem):
    return [
        pltpu.make_async_copy(
            tokens_ref.at[:, pl.ds(pl.multiple_of((piece * PLANE + column) * run, run), run)],
            out.at[piece],
            sem,
        )
        for piece in range(out.shape[0])
    ]


def choose_kernel(
    planes, entry_hbm, adapter_hbm, counts_hbm, tokens_ref, down_ref, up_ref, table_ref, *refs
):
    others = planes - 1
    sends, tokens_out = refs[:others], refs[others : others + PLANE - 2]
    entry_ref, adapter_ref, counts_ref, held_ref, small_sem, tokens_sem, sem = refs[others + PLANE - 2 :]
    me = lax.axis_index("wide")
    column, plane = lax.rem(me, PLANE), lax.div(me, PLANE)
    run, up_run = down_ref.shape[2], up_ref.shape[2]
    small = [
        pltpu.make_async_copy(entry_hbm, entry_ref, small_sem.at[0]),
        pltpu.make_async_copy(adapter_hbm, adapter_ref, small_sem.at[1]),
        pltpu.make_async_copy(counts_hbm, counts_ref, small_sem.at[2]),
    ]
    for copy in small:
        copy.start()
    for k, out in enumerate(tokens_out):
        for copy in slices(tokens_ref, column ^ (k + 2), run, out, tokens_sem.at[k]):
            copy.start()
    for copy in small:
        copy.wait()

    requests = counts_ref.shape[0]
    ends, total = [], 0
    for q in range(requests):
        total = total + counts_ref[q]
        ends.append(total)
    entries = [entry_ref[adapter_ref[q]] for q in range(requests)]

    def listed(p):
        ids = []
        for i in range(PLANE):
            block = p * PLANE + jnp.where(p % 2 == 0, i, PLANE - 1 - i)
            got = entries[0]
            for q in range(1, requests):
                got = jnp.where(ends[q - 1] <= block, entries[q], got)
            ids.append(got)
        place, held, count = [jnp.int32(0)], [ids[0]] * SLOTS, jnp.int32(1)
        for i in range(1, PLANE):
            found = count
            for j in range(i):
                found = jnp.where(ids[i] == ids[j], place[j], found)
            place.append(found)
            held = [jnp.where(found == s, ids[i], held[s]) for s in range(SLOTS)]
            count = jnp.maximum(count, found + 1)
        return held, place, count

    most = jnp.int32(1)
    for d in (*range(2, planes), 1, 0):
        held, place, count = listed(plane ^ d)
        most = jnp.maximum(most, count)
        if d > 0:
            for s in range(sends[d - 1].shape[0]):
                out = sends[d - 1].at[s]
                for ref, at in (down_ref, pl.ds(0, run)), (up_ref, pl.ds(run, up_run)):
                    pltpu.make_async_copy(ref.at[held[s]], out.at[:, at], sem.at[d - 1]).start()
        else:
            for s in range(SLOTS):
                held_ref[PLANE + s] = held[s]
    for k in range(PLANE):
        i = column ^ k
        held_ref[k] = pick(jnp.where(plane % 2 == 0, i, PLANE - 1 - i), place)
    held_ref[PLANE + SLOTS] = jnp.where(most > USUAL, 1, 0)
    table = pltpu.make_async_copy(held_ref, table_ref, small_sem.at[3])
    table.start()
    for k, out in enumerate(tokens_out):
        landed(out, tokens_sem.at[k])
    for d, out in enumerate(sends):
        landed(out, sem.at[d])
    table.wait()


def choose(planes, tokens, down, up, entry, adapter, counts):
    hbm = pl.BlockSpec(memory_space=pltpu.HBM)
    others = planes - 1
    rows = (2, down.shape[2] + up.shape[2], down.shape[3])
    sends = [
        jax.ShapeDtypeStruct((SLOTS if d == 1 else USUAL,) + rows, down.dtype) for d in range(1, planes)
    ]
    return pl.pallas_call(
        lambda *refs: choose_kernel(planes, *refs),
        out_shape=[jax.ShapeDtypeStruct((PLANE + SLOTS + 1,), jnp.int32)]
        + sends
        + [jax.ShapeDtypeStruct((2 * planes, BLK, down.shape[2]), tokens.dtype)] * (PLANE - 2),
        in_specs=[hbm] * 6,
        out_specs=[pl.BlockSpec(memory_space=pl.ANY)]
        + [pl.BlockSpec(memory_space=pltpu.VMEM)] * (others + PLANE - 2),
        scratch_shapes=[
            pltpu.SMEM(entry.shape, jnp.int32),
            pltpu.SMEM(adapter.shape, jnp.int32),
            pltpu.SMEM(counts.shape, jnp.int32),
            pltpu.SMEM((PLANE + SLOTS + 1,), jnp.int32),
            pltpu.SemaphoreType.DMA((4,)),
            pltpu.SemaphoreType.DMA((PLANE - 2,)),
            pltpu.SemaphoreType.DMA((others,)),
        ],
        compiler_params=pltpu.CompilerParams(vmem_limit_bytes=57 * 2**20),
        name="choose",
    )(entry, adapter, counts, tokens, down, up)


def gather_kernel(planes, table_ref, tokens_ref, down_ref, up_ref, own_ref, pair_ref, tokens_sem, sem):
    column = lax.rem(lax.axis_index("wide"), PLANE)
    run, up_run = down_ref.shape[2], up_ref.shape[2]
    for core in range(2):
        at = lax.div(column, 2) * 2 + core
        for copy in slices(tokens_ref, at, run, pair_ref.at[core], tokens_sem.at[core]):
            copy.start()
    for s in range(SLOTS):
        slot = table_ref[PLANE + s]
        for ref, rows in (down_ref, pl.ds(0, run)), (up_ref, pl.ds(run, up_run)):
            pltpu.make_async_copy(ref.at[slot], own_ref.at[s, :, rows], sem).start()
    for core in range(2):
        landed(pair_ref.at[core], tokens_sem.at[core])
    landed(own_ref, sem)


def gather(planes, table, tokens, down, up):
    run = down.shape[2]
    hbm = pl.BlockSpec(memory_space=pltpu.HBM)
    rows = (2, run + up.shape[2], down.shape[3])
    return pl.pallas_call(
        lambda *refs: gather_kernel(planes, *refs),
        out_shape=[
            jax.ShapeDtypeStruct((SLOTS,) + rows, down.dtype),
        ]
        + [jax.ShapeDtypeStruct((2, 2 * planes, BLK, run), tokens.dtype)],
        in_specs=[pl.BlockSpec(memory_space=pltpu.SMEM)] + [hbm] * 3,
        out_specs=[pl.BlockSpec(memory_space=pltpu.VMEM)] * 2,
        scratch_shapes=[
            pltpu.SemaphoreType.DMA((2,)),
            pltpu.SemaphoreType.DMA(()),
        ],
        compiler_params=pltpu.CompilerParams(vmem_limit_bytes=57 * 2**20),
        name="gather",
    )(table, tokens, down, up)


def up_rows(factors, distances, place):
    rows = []
    for d in distances:
        slot = jnp.minimum(place, factors[d].shape[0] - 1)
        rows += [factors[d][slot, half] for half in range(2)]
    return rows


def shrink(
    planes,
    slots,
    run,
    blocks,
    near,
    first,
    far,
    places,
    rows,
    factors,
    held=(),
    ups=None,
    flops=None,
    kept=(),
    flag=False,
):
    vmem, smem = pl.BlockSpec(memory_space=pltpu.VMEM), pl.BlockSpec(memory_space=pltpu.SMEM)
    up_run, ranks = factors[0].shape[2] - run, factors[0].shape[3]

    used = sorted({*first, *far})

    def kernel(places_ref, *refs):
        spread = len(places.shape) > 1
        row_refs, refs = refs[: len(rows)], refs[len(rows) :]
        factor_refs, refs = dict(zip(used, refs)), refs[len(used) :]
        held_refs, outs = list(refs[: len(held)]), refs[len(held) + len(kept) :]
        me = lax.axis_index("wide")
        core, plane = lax.rem(me, 2), lax.div(me, PLANE)
        at = [places_ref[k, pl.ds(0, 1)] if spread else places_ref[k] for k in blocks]
        views = {d: ref.at[:, :, pl.ds(run, up_run)] for d, ref in factor_refs.items()}

        def rows_of_up(place):
            if not spread:
                return up_rows(views, ups or (), place)
            return [
                pick(place, [views[d][s, half].astype(jnp.float32) for s in range(slots)])
                for d in ups or ()
                for half in range(2)
            ]

        def rows_at(k, piece):
            return row_refs[0][core ^ k, piece] if k < 2 else row_refs[k - 1][piece]

        def sums_of(chosen, distances):
            total = jnp.zeros((len(chosen) * BLK, slots * ranks), jnp.float32)
            for d in distances:
                for half in range(2):
                    piece = half * planes + (plane ^ d)
                    total += jnp.dot(
                        jnp.concatenate([rows_at(blocks[i], piece) for i in chosen], axis=0),
                        jnp.concatenate(
                            [factor_refs[d][s, half, pl.ds(0, run)] for s in range(slots)], axis=1
                        ),
                        preferred_element_type=jnp.float32,
                    )
            parts = [total[j * BLK : (j + 1) * BLK] for j in range(len(chosen))]
            return {
                i: pick(at[i], [part[:, s * ranks : (s + 1) * ranks] for s in range(slots)])
                for i, part in zip(chosen, parts)
            }

        if flag:
            *outs, spread_ref, flag_ref = outs
            flag_ref[0] = places_ref[PLANE + SLOTS]
            for k in range(PLANE):
                spread_ref[k] = jnp.full(spread_ref.shape[1:], places_ref[k], jnp.int32)
        every = range(len(blocks))
        mine = sums_of(every, far) if far else {}
        here = [i for i in every if blocks[i] in near]
        for i, part in (sums_of(here, first) if here else {}).items():
            mine[i] = mine[i] + part if far else part
        for i in every:
            if i not in here:
                mine[i] = mine[i] + held_refs.pop(0)[...]
            outs[i][pl.ds(0, BLK)] = mine[i].astype(outs[i].dtype)
            for j, part in enumerate(rows_of_up(at[i])):
                outs[i][pl.ds(BLK + j * up_run, up_run)] = part.astype(outs[i].dtype)

    height = BLK + len(ups or ()) * 2 * up_run
    exact = [ups is None or k == 0 for k in blocks]
    cost = None
    if flops is not None:
        cost = pl.CostEstimate(flops=flops, bytes_accessed=0, transcendentals=0)
    return pl.pallas_call(
        kernel,
        out_shape=[
            jax.ShapeDtypeStruct((height, ranks), jnp.float32 if full else rows[0].dtype)
            for full in exact
        ]
        + [jax.ShapeDtypeStruct((PLANE, 8, ranks), jnp.int32), jax.ShapeDtypeStruct((1,), jnp.int32)]
        * flag,
        in_specs=[vmem if len(places.shape) > 1 else smem]
        + [vmem] * (len(rows) + len(used) + len(held))
        + [pl.BlockSpec(memory_space=pl.ANY)] * len(kept),
        out_specs=[vmem] * len(blocks) + [vmem, smem] * flag,
        compiler_params=pltpu.CompilerParams(vmem_limit_bytes=10 * 2**20),
        cost_estimate=cost,
        name="shrink",
    )(places, *rows, *[factors[d] for d in used], *held, *kept)


def expand(planes, up_run, sums):
    ranks = sums[0].shape[1]
    columns = 2 * planes * PLANE * up_run
    vmem = pl.BlockSpec(memory_space=pltpu.VMEM)
    span = 2 * up_run
    order = (2, 3, 1, 0)

    def kernel(*refs):
        sum_refs = dict(zip(order, refs))
        key_ref, value_ref, factor = refs[PLANE:]
        me = lax.axis_index("wide")
        column, plane = lax.rem(me, PLANE), lax.div(me, PLANE)
        total = jnp.zeros((BLK, ranks), jnp.float32)
        for k in range(PLANE):
            total += sum_refs[k][pl.ds(0, BLK)].astype(jnp.float32)
            for d in range(planes):
                rows = sum_refs[k][pl.ds(BLK + d * span, span)]
                factor[plane ^ d, :, column ^ k] = rows.astype(factor.dtype).reshape(2, up_run, ranks)
        low_rank = total.astype(jnp.bfloat16)
        is_key = lax.broadcasted_iota(jnp.int32, low_rank.shape, 1) < ranks // 2
        zero = jnp.zeros_like(low_rank)
        both = jnp.concatenate(
            [jnp.where(is_key, low_rank, zero), jnp.where(is_key, zero, low_rank)], axis=0
        )
        for half in range(2):
            for p in range(planes):
                delta = lax.dot_general(
                    both,
                    factor[p, half].reshape(PLANE * up_run, ranks),
                    (((1,), (1,)), ((), ())),
                    preferred_element_type=jnp.float32,
                ).astype(jnp.bfloat16)
                at = pl.ds((half * planes + p) * PLANE * up_run, PLANE * up_run)
                key_ref[:, at] = delta[:BLK]
                value_ref[:, at] = delta[BLK:]

    return pl.pallas_call(
        kernel,
        out_shape=[jax.ShapeDtypeStruct((BLK, columns), jnp.bfloat16)] * 2,
        in_specs=[vmem] * PLANE,
        out_specs=[vmem] * 2,
        scratch_shapes=[pltpu.VMEM((planes, 2, PLANE, up_run, ranks), jnp.bfloat16)],
        compiler_params=pltpu.CompilerParams(vmem_limit_bytes=4 * 2**20),
        name="expand",
    )(*[sums[k] for k in order])


def plane_body(
    tokens,
    adapter_down_weight,
    adapter_up_weight,
    adapter_entry,
    adapter_of_request,
    token_blocks_per_request,
):
    planes = lax.axis_size("wide") // PLANE
    places, *sends = choose(
        planes,
        tokens,
        adapter_down_weight,
        adapter_up_weight,
        adapter_entry,
        adapter_of_request,
        token_blocks_per_request,
    )
    factors, across = sends[: planes - 1], sends[planes - 1 :]
    own_factors, pair = gather(planes, places, tokens, adapter_down_weight, adapter_up_weight)
    sends = sends + [pair]
    run, up_run = adapter_down_weight.shape[2], adapter_up_weight.shape[2]
    whole, blocks = tuple(range(planes)), tuple(range(PLANE))
    factors = [own_factors] + [swap(factors[d - 1], d * PLANE) for d in whole[1:]]
    rows = [swap_cores(pair)] + [swap(across[k - 2], k) for k in range(2, PLANE)]
    early = (0, 2)
    *held, spread, many = shrink(
        planes,
        USUAL,
        run,
        blocks[:2],
        blocks[:2],
        early,
        (),
        places,
        rows[:1],
        factors,
        flops=3*10**9,
        flag=True,
    )

    def finish(sums):
        sums = [sums[0]] + [swap(sums[k], k) for k in range(1, PLANE)]
        return tuple(expand(planes, up_run, sums))

    def usual(places, spread, factors, rows, held, kept):
        args = (early, (1, 3), spread, rows, factors)
        sums = shrink(planes, USUAL, run, blocks[1:], blocks[2:], *args, held[1:], whole)
        return finish([*shrink(planes, USUAL, run, blocks[:1], (), *args, held[:1], whole), *sums])

    def more(places, spread, factors, rows, held, kept):
        third = [swap(factors[d ^ 1][:1], PLANE) for d in whole[2:]]
        factors = factors[:2] + [jnp.concatenate([factors[d], third[d - 2]]) for d in whole[2:]]
        sums = shrink(
            planes, SLOTS, run, blocks, blocks, whole, (), places, rows, factors, (), whole, kept=kept
        )
        return finish(sums)

    return lax.switch(many[0], [usual, more], places, spread, factors, rows, held, sends)


def solution(mesh):
    by_plane = mesh.shape["wide"] == 16 and mesh.shape["narrow"] == 1
    return jax.shard_map(
        plane_body if by_plane else direct_body,
        mesh=mesh,
        in_specs=(
            P(("groups", "wide"), "narrow"),
            P(None, "narrow", "wide", None),
            P(None, "narrow", "wide", None),
            P(),
            P("groups"),
            P("groups"),
        ),
        out_specs=(P(("groups", "wide"), "narrow"), P(("groups", "wide"), "narrow")),
        check_vma=False,
    )
```

profile of v0, /device:TPU:21, one launch (start us, length us, event | category | flops | bytes accessed | tf_op | source)
XLA Modules:
  0.0 50.5 jit_solution(2557409360822112693)
XLA Ops:
  0.6 2.3 %choose.1 = (s32[8]{0:T(128)S(1)}, bf16[3,2,288,128]{3,2,1,0:T(8,128)(2,1)S(1)}, bf16[2,2,288,128]{3,2,1,0:T(8,128)(2,1)S(1)}, bf16[2,2,288,128]{3,2,1,0:T(8,128...) custom-call(s32[16]{0:T(128)} %refs_0_.1, s32[4]{0:T(128)} %refs_1_.2, s32[4]{0:T(128)} %refs_2_.2, ...), custom_call_target="tpu_custom_call" | custom-call | tf_op jit(solution)/shard_map/choose/pallas_call | solution.py:198
  2.9 0.1 collective-permute-start.8
  3.0 1.2 %collective-permute-start.9 = (bf16[8,128,256]{2,1,0:T(8,128)(2,1)S(1)}, bf16[8,128,256]{2,1,0:T(8,128)(2,1)S(1)}, u32[]{:S(2)}, u32[]{:S(2)}) collective-permute-start(bf16[8,128,256]{2,1,0:T(8,128)(2,1)S(1)} %get-tuple-element.99), channel_id=1, source_target_pairs={{0,2},{1,3},{2,0},{3,1},{4,6},{5,7},{6,4},{7,5},{8,10},{9,11},{10,... | collective-permute-start | bytes 1572872 | tf_op jit(solution)/shard_map/ppermute | solution.py:88
  4.3 1.4 %collective-permute-start.10 = (bf16[8,128,256]{2,1,0:T(8,128)(2,1)S(1)}, bf16[8,128,256]{2,1,0:T(8,128)(2,1)S(1)}, u32[]{:S(2)}, u32[]{:S(2)}) collective-permute-start(bf16[8,128,256]{2,1,0:T(8,128)(2,1)S(1)} %get-tuple-element.100), channel_id=1, source_target_pairs={{0,3},{1,2},{2,1},{3,0},{4,7},{5,6},{6,5},{7,4},{8,11},{9,10},{10,... | collective-permute-start | bytes 1572872 | tf_op jit(solution)/shard_map/ppermute | solution.py:88
  5.6 1.3 %collective-permute-start.11 = (bf16[3,2,288,128]{3,2,1,0:T(8,128)(2,1)S(1)}, bf16[3,2,288,128]{3,2,1,0:T(8,128)(2,1)S(1)}, u32[]{:S(2)}, u32[]{:S(2)}) collective-permute-start(bf16[3,2,288,128]{3,2,1,0:T(8,128)(2,1)S(1)} %get-tuple-element.101), channel_id=1, source_target_pairs={{0,4},{1,5},{2,6},{3,7},{4,0},{5,1},{6,2},{7,3},{8,12},{9,13},{10,... | collective-permute-start | bytes 1327112 | tf_op jit(solution)/shard_map/ppermute | solution.py:88
  6.9 1.3 %collective-permute-start.12 = (bf16[2,2,288,128]{3,2,1,0:T(8,128)(2,1)S(1)}, bf16[2,2,288,128]{3,2,1,0:T(8,128)(2,1)S(1)}, u32[]{:S(2)}, u32[]{:S(2)}) collective-permute-start(bf16[2,2,288,128]{3,2,1,0:T(8,128)(2,1)S(1)} %get-tuple-element.102), channel_id=1, source_target_pairs={{0,12},{1,13},{2,14},{3,15},{4,8},{5,9},{6,10},{7,11},{8,4},{9,5},... | collective-permute-start | bytes 884744 | tf_op jit(solution)/shard_map/ppermute | solution.py:88
  8.2 2.0 %gather.1 = (bf16[3,2,288,128]{3,2,1,0:T(8,128)(2,1)S(1)}, bf16[2,8,128,256]{3,2,1,0:T(8,128)(2,1)S(1)}) custom-call(s32[8]{0:T(128)S(1)} %get-tuple-element.93.refs_0_.places_ref, bf16[128,8192]{1,0:T(8,128)(2,1)} %refs_1_.3, bf16[16,2,256,128]{3,2,1,0:T(8,128)(2,1)} %refs_2_.3, bf16[16,2,32,128]{3,2,1,0:T(8,128)(2,1)} %refs_3_.3), custom_call_target="tpu_custom_call" | custom-call | tf_op jit(solution)/shard_map/gather/pallas_call | solution.py:240
  10.2 4.6 %all_to_all.5.refs_0_ = bf16[2,8,128,256]{3,2,1,0:T(8,128)(2,1)S(1)} all-to-all(bf16[2,8,128,256]{3,2,1,0:T(8,128)(2,1)S(1)} %get-tuple-element.94), channel_id=1, replica_groups={{0,1},{2,3},{4,5},{6,7},{8,9},{10,11},{12,13},{14,15},{16,17},{18,19},{..., dimensions={0} | all-to-all | bytes 2097152 | tf_op jit(solution)/shard_map/all_to_all | solution.py:94
  14.9 0.2 collective-permute-done.8.refs_2_
  15.1 1.2 %shrink.7 = (f32[128,128]{1,0:T(8,128)S(1)}, f32[128,128]{1,0:T(8,128)S(1)}, s32[4,8,128]{2,1,0:T(8,128)S(1)}, s32[1]{0:T(128)}) custom-call(s32[8]{0:T(128)S(1)} %get-tuple-element.93.refs_0_.places_ref, bf16[2,8,128,256]{3,2,1,0:T(8,128)(2,1)S(1)} %all_to_all.5.refs_0_, bf16[3,2,288,128]{3,2,1,0:T(8,128)(2,1)S(1)} %get-tuple-element.95.refs_1_, ...), custom_call_target="tpu_custom_call" | custom-call | flops 3000000000 | tf_op jit(solution)/shard_map/shrink/pallas_call | solution.py:349
  16.9 14.9 %collective-permute-done.12 = bf16[2,2,288,128]{3,2,1,0:T(8,128)(2,1)S(1)} collective-permute-done((bf16[2,2,288,128]{3,2,1,0:T(8,128)(2,1)S(1)}, bf16[2,2,288,128]{3,2,1,0:T(8,128)(2,1)S(1)}, u32[]{:S(2)}, u32[]{:S(2)}) %collective-permute-start.12) | collective-permute-done | bytes 294944 | tf_op jit(solution)/shard_map/ppermute | solution.py:88
  31.8 0.0 collective-permute-done.11
  31.8 0.0 collective-permute-done.9
  31.8 0.0 collective-permute-done.10
  31.8 18.7 %conditional.1 = ((bf16[128,1024]{1,0:T(8,128)(2,1)}, bf16[128,1024]{1,0:T(8,128)(2,1)})) conditional(s32[]{:T(128)} %bitcast, (s32[4,8,128]{2,1,0:T(8,128)S(1)}, bf16[2,8,128,256]{3,2,1,0:T(8,128)(2,1)S(1)}, bf16[8,128,256]{2,1,0:T(8,128)(2,1)S(1)}, bf16[8,128,256]{2,1,0:T(8,128)(2,1)S(1)}, bf16[3,2,288,128]{3,2,1,0:T(8,128)(2,1)S(1)}, ...), branch_computations={%region_0.0_spmd, %region_1.0_spmd} | conditional | flops 442368 | bytes 4718800 | solution.py:472
  31.9 0.1 collective-permute-start.3
  32.0 1.5 %collective-permute-start.4 = (bf16[1,2,288,128]{3,2,1,0:T(8,128)(2,1)S(1)}, bf16[1,2,288,128]{3,2,1,0:T(8,128)(2,1)S(1)}, u32[]{:S(2)}, u32[]{:S(2)}) collective-permute-start(bf16[1,2,288,128]{3,2,1,0:T(8,128)(2,1)S(1)} %slice.5), channel_id=1, source_target_pairs={{0,4},{1,5},{2,6},{3,7},{4,0},{5,1},{6,2},{7,3},{8,12},{9,13},{10,... | collective-permute-start | bytes 442376 | tf_op jit(solution)/shard_map/cond/branch_1_fun/ppermute | solution.py:88
  33.5 3.4 %collective-permute-done.3 = bf16[1,2,288,128]{3,2,1,0:T(8,128)(2,1)S(1)} collective-permute-done((bf16[1,2,288,128]{3,2,1,0:T(8,128)(2,1)S(1)}, bf16[1,2,288,128]{3,2,1,0:T(8,128)(2,1)S(1)}, u32[]{:S(2)}, u32[]{:S(2)}) %collective-permute-start.3) | collective-permute-done | bytes 147488 | tf_op jit(solution)/shard_map/cond/branch_1_fun/ppermute | solution.py:88
  36.9 3.1 %collective-permute-done.4 = bf16[1,2,288,128]{3,2,1,0:T(8,128)(2,1)S(1)} collective-permute-done((bf16[1,2,288,128]{3,2,1,0:T(8,128)(2,1)S(1)}, bf16[1,2,288,128]{3,2,1,0:T(8,128)(2,1)S(1)}, u32[]{:S(2)}, u32[]{:S(2)}) %collective-permute-start.4) | collective-permute-done | bytes 147488 | tf_op jit(solution)/shard_map/cond/branch_1_fun/ppermute | solution.py:88
  40.1 1.8 %shrink.6 = (f32[384,128]{1,0:T(8,128)S(1)}, bf16[384,128]{1,0:T(8,128)(2,1)S(1)}, bf16[384,128]{1,0:T(8,128)(2,1)S(1)}, bf16[384,128]{1,0:T(8,128)(2,1)S(1)}) custom-call(s32[8]{0:T(128)S(1)} %get-tuple-element.61.places_ref, bf16[2,8,128,256]{3,2,1,0:T(8,128)(2,1)S(1)} %get-tuple-element.62.refs_0_, bf16[8,128,256]{2,1,0:T(8,128)(2,1)S(1)} %get-tuple-element.63.refs_1_, ...), custom_call_target="tpu_custom_call" | custom-call | tf_op jit(solution)/shard_map/cond/branch_1_fun/shrink/pallas_call | solution.py:349
  41.9 1.3 %collective-permute-start.5 = (bf16[384,128]{1,0:T(8,128)(2,1)S(1)}, bf16[384,128]{1,0:T(8,128)(2,1)S(1)}, u32[]{:S(2)}, u32[]{:S(2)}) collective-permute-start(bf16[384,128]{1,0:T(8,128)(2,1)S(1)} %get-tuple-element.75), channel_id=1, source_target_pairs={{0,2},{1,3},{2,0},{3,1},{4,6},{5,7},{6,4},{7,5},{8,10},{9,11},{10,... | collective-permute-start | bytes 294920 | tf_op jit(solution)/shard_map/cond/branch_1_fun/ppermute | solution.py:88
  43.1 1.8 %collective-permute-start.6 = (bf16[384,128]{1,0:T(8,128)(2,1)S(1)}, bf16[384,128]{1,0:T(8,128)(2,1)S(1)}, u32[]{:S(2)}, u32[]{:S(2)}) collective-permute-start(bf16[384,128]{1,0:T(8,128)(2,1)S(1)} %get-tuple-element.76), channel_id=1, source_target_pairs={{0,3},{1,2},{2,1},{3,0},{4,7},{5,6},{6,5},{7,4},{8,11},{9,10},{10,... | collective-permute-start | bytes 294920 | tf_op jit(solution)/shard_map/cond/branch_1_fun/ppermute | solution.py:88
  44.9 0.0 collective-permute-start.7
  44.9 0.5 collective-permute-done.5.refs_0_
  45.4 4.0 %collective-permute-done.6.refs_1_ = bf16[384,128]{1,0:T(8,128)(2,1)S(1)} collective-permute-done((bf16[384,128]{1,0:T(8,128)(2,1)S(1)}, bf16[384,128]{1,0:T(8,128)(2,1)S(1)}, u32[]{:S(2)}, u32[]{:S(2)}) %collective-permute-start.6) | collective-permute-done | bytes 98336 | tf_op jit(solution)/shard_map/cond/branch_1_fun/ppermute | solution.py:88
  49.4 0.0 collective-permute-done.7.refs_2_
  49.4 1.1 %expand.3 = (bf16[128,1024]{1,0:T(8,128)(2,1)}, bf16[128,1024]{1,0:T(8,128)(2,1)}) custom-call(bf16[384,128]{1,0:T(8,128)(2,1)S(1)} %collective-permute-done.5.refs_0_, bf16[384,128]{1,0:T(8,128)(2,1)S(1)} %collective-permute-done.6.refs_1_, bf16[384,128]{1,0:T(8,128)(2,1)S(1)} %collective-permute-done.7.refs_2_, f32[384,128]{1,0:T(8,128)S(1)} %get-tuple-element.78.refs_3_), custom_call_target="tpu_custom_call" | custom-call | tf_op jit(solution)/shard_map/cond/branch_1_fun/expand/pallas_call | solution.py:403
  (4 shorter events, 0.1 us)
Async XLA Ops:
  2.9 12.2 %collective-permute-start.8 = (bf16[2,2,288,128]{3,2,1,0:T(8,128)(2,1)S(1)}, bf16[2,2,288,128]{3,2,1,0:T(8,128)(2,1)S(1)}, u32[]{:S(2)}, u32[]{:S(2)}) collective-permute-start(bf16[2,2,288,128]{3,2,1,0:T(8,128)(2,1)S(1)} %get-tuple-element.96), channel_id=1, source_target_pairs={{0,8},{1,9},{2,10},{3,11},{4,12},{5,13},{6,14},{7,15},{8,0},{9,1},... | collective-permute-start | bytes 884744 | tf_op jit(solution)/shard_map/ppermute | solution.py:88
  3.0 28.8 %collective-permute-start.9 = (bf16[8,128,256]{2,1,0:T(8,128)(2,1)S(1)}, bf16[8,128,256]{2,1,0:T(8,128)(2,1)S(1)}, u32[]{:S(2)}, u32[]{:S(2)}) collective-permute-start(bf16[8,128,256]{2,1,0:T(8,128)(2,1)S(1)} %get-tuple-element.99), channel_id=1, source_target_pairs={{0,2},{1,3},{2,0},{3,1},{4,6},{5,7},{6,4},{7,5},{8,10},{9,11},{10,... | collective-permute-start | bytes 1572872 | tf_op jit(solution)/shard_map/ppermute | solution.py:88
  4.3 27.6 %collective-permute-start.10 = (bf16[8,128,256]{2,1,0:T(8,128)(2,1)S(1)}, bf16[8,128,256]{2,1,0:T(8,128)(2,1)S(1)}, u32[]{:S(2)}, u32[]{:S(2)}) collective-permute-start(bf16[8,128,256]{2,1,0:T(8,128)(2,1)S(1)} %get-tuple-element.100), channel_id=1, source_target_pairs={{0,3},{1,2},{2,1},{3,0},{4,7},{5,6},{6,5},{7,4},{8,11},{9,10},{10,... | collective-permute-start | bytes 1572872 | tf_op jit(solution)/shard_map/ppermute | solution.py:88
  5.6 26.2 %collective-permute-start.11 = (bf16[3,2,288,128]{3,2,1,0:T(8,128)(2,1)S(1)}, bf16[3,2,288,128]{3,2,1,0:T(8,128)(2,1)S(1)}, u32[]{:S(2)}, u32[]{:S(2)}) collective-permute-start(bf16[3,2,288,128]{3,2,1,0:T(8,128)(2,1)S(1)} %get-tuple-element.101), channel_id=1, source_target_pairs={{0,4},{1,5},{2,6},{3,7},{4,0},{5,1},{6,2},{7,3},{8,12},{9,13},{10,... | collective-permute-start | bytes 1327112 | tf_op jit(solution)/shard_map/ppermute | solution.py:88
  6.9 24.9 %collective-permute-start.12 = (bf16[2,2,288,128]{3,2,1,0:T(8,128)(2,1)S(1)}, bf16[2,2,288,128]{3,2,1,0:T(8,128)(2,1)S(1)}, u32[]{:S(2)}, u32[]{:S(2)}) collective-permute-start(bf16[2,2,288,128]{3,2,1,0:T(8,128)(2,1)S(1)} %get-tuple-element.102), channel_id=1, source_target_pairs={{0,12},{1,13},{2,14},{3,15},{4,8},{5,9},{6,10},{7,11},{8,4},{9,5},... | collective-permute-start | bytes 884744 | tf_op jit(solution)/shard_map/ppermute | solution.py:88
  31.9 5.0 %collective-permute-start.3 = (bf16[1,2,288,128]{3,2,1,0:T(8,128)(2,1)S(1)}, bf16[1,2,288,128]{3,2,1,0:T(8,128)(2,1)S(1)}, u32[]{:S(2)}, u32[]{:S(2)}) collective-permute-start(bf16[1,2,288,128]{3,2,1,0:T(8,128)(2,1)S(1)} %slice.4), channel_id=1, source_target_pairs={{0,4},{1,5},{2,6},{3,7},{4,0},{5,1},{6,2},{7,3},{8,12},{9,13},{10,... | collective-permute-start | bytes 442376 | tf_op jit(solution)/shard_map/cond/branch_1_fun/ppermute | solution.py:88
  32.0 8.1 %collective-permute-start.4 = (bf16[1,2,288,128]{3,2,1,0:T(8,128)(2,1)S(1)}, bf16[1,2,288,128]{3,2,1,0:T(8,128)(2,1)S(1)}, u32[]{:S(2)}, u32[]{:S(2)}) collective-permute-start(bf16[1,2,288,128]{3,2,1,0:T(8,128)(2,1)S(1)} %slice.5), channel_id=1, source_target_pairs={{0,4},{1,5},{2,6},{3,7},{4,0},{5,1},{6,2},{7,3},{8,12},{9,13},{10,... | collective-permute-start | bytes 442376 | tf_op jit(solution)/shard_map/cond/branch_1_fun/ppermute | solution.py:88
  41.9 3.5 %collective-permute-start.5 = (bf16[384,128]{1,0:T(8,128)(2,1)S(1)}, bf16[384,128]{1,0:T(8,128)(2,1)S(1)}, u32[]{:S(2)}, u32[]{:S(2)}) collective-permute-start(bf16[384,128]{1,0:T(8,128)(2,1)S(1)} %get-tuple-element.75), channel_id=1, source_target_pairs={{0,2},{1,3},{2,0},{3,1},{4,6},{5,7},{6,4},{7,5},{8,10},{9,11},{10,... | collective-permute-start | bytes 294920 | tf_op jit(solution)/shard_map/cond/branch_1_fun/ppermute | solution.py:88
  43.1 6.3 %collective-permute-start.6 = (bf16[384,128]{1,0:T(8,128)(2,1)S(1)}, bf16[384,128]{1,0:T(8,128)(2,1)S(1)}, u32[]{:S(2)}, u32[]{:S(2)}) collective-permute-start(bf16[384,128]{1,0:T(8,128)(2,1)S(1)} %get-tuple-element.76), channel_id=1, source_target_pairs={{0,3},{1,2},{2,1},{3,0},{4,7},{5,6},{6,5},{7,4},{8,11},{9,10},{10,... | collective-permute-start | bytes 294920 | tf_op jit(solution)/shard_map/cond/branch_1_fun/ppermute | solution.py:88
  44.9 4.5 %collective-permute-start.7 = (bf16[384,128]{1,0:T(8,128)(2,1)S(1)}, bf16[384,128]{1,0:T(8,128)(2,1)S(1)}, u32[]{:S(2)}, u32[]{:S(2)}) collective-permute-start(bf16[384,128]{1,0:T(8,128)(2,1)S(1)} %get-tuple-element.77), channel_id=1, source_target_pairs={{0,1},{1,0},{2,3},{3,2},{4,5},{5,4},{6,7},{7,6},{8,9},{9,8},{10,11... | collective-permute-start | bytes 294920 | tf_op jit(solution)/shard_map/cond/branch_1_fun/ppermute | solution.py:88
where the time goes:
time: 50.8 us; the launch traced here: 50.5 us
  waiting for transfers between devices  26.2 us (52%)
  starting transfers between devices  9.94 us (20%)
  Pallas kernels  8.32 us (16%)
  blocking collectives  4.64 us (9%)
  between operations  1.31 us (3%)
    ppermute x10, waiting for transfers between devices, swap(): return lax.ppermute(value, 'wide', [(i, i ^ step) for i in range(count)])  26.2 us
    ppermute x10, starting transfers between devices, swap(): return lax.ppermute(value, 'wide', [(i, i ^ step) for i in range(count)])  9.94 us
    all_to_all x1, blocking collectives, swap_cores(): lax.all_to_all(value, 'wide', 0, 0, axis_index_groups=pairs, tiled=True)  4.64 us
    pallas_call x2, Pallas kernels, shrink(): pl.pallas_call(kernel, out_shape=[jax.ShapeDtypeStruct((height, ranks), j...  2.95 us
    pallas_call x1, Pallas kernels, choose(): pl.pallas_call(lambda *refs: choose_kernel(planes, *refs), out_shape=[jax...  2.27 us
    pallas_call x1, Pallas kernels, gather(): pl.pallas_call(lambda *refs: gather_kernel(planes, *refs), out_shape=[jax...  1.99 us
    pallas_call x1, Pallas kernels, expand(): pl.pallas_call(kernel, out_shape=[jax.ShapeDtypeStruct((BLK, columns), jn...  1.11 us
  transfers between devices with their start and end apart: 10, of which 6 were waited for; matrix products, arithmetic and copies ran while one was open for 0% of the time, Pallas kernels for 6%

commit v1 on v0

--- a/solution.py
+++ b/solution.py
@@ -276,7 +276,6 @@
     held=(),
     ups=None,
     flops=None,
-    kept=(),
     flag=False,
 ):
     vmem, smem = pl.BlockSpec(memory_space=pltpu.VMEM), pl.BlockSpec(memory_space=pltpu.SMEM)
@@ -288,7 +287,7 @@
         spread = len(places.shape) > 1
         row_refs, refs = refs[: len(rows)], refs[len(rows) :]
         factor_refs, refs = dict(zip(used, refs)), refs[len(used) :]
-        held_refs, outs = list(refs[: len(held)]), refs[len(held) + len(kept) :]
+        held_refs, outs = list(refs[: len(held)]), refs[len(held) :]
         me = lax.axis_index("wide")
         core, plane = lax.rem(me, 2), lax.div(me, PLANE)
         at = [places_ref[k, pl.ds(0, 1)] if spread else places_ref[k] for k in blocks]
@@ -355,13 +354,56 @@
         + [jax.ShapeDtypeStruct((PLANE, 8, ranks), jnp.int32), jax.ShapeDtypeStruct((1,), jnp.int32)]
         * flag,
         in_specs=[vmem if len(places.shape) > 1 else smem]
-        + [vmem] * (len(rows) + len(used) + len(held))
-        + [pl.BlockSpec(memory_space=pl.ANY)] * len(kept),
+        + [vmem] * (len(rows) + len(used) + len(held)),
         out_specs=[vmem] * len(blocks) + [vmem, smem] * flag,
         compiler_params=pltpu.CompilerParams(vmem_limit_bytes=10 * 2**20),
         cost_estimate=cost,
         name="shrink",
-    )(places, *rows, *[factors[d] for d in used], *held, *kept)
+    )(places, *rows, *[factors[d] for d in used], *held)
+
+
+def amend(planes, run, places, rows, thirds, slots, sums, kept):
+    vmem = pl.BlockSpec(memory_space=pltpu.VMEM)
+    up_run, ranks = thirds[0].shape[2] - run, thirds[0].shape[3]
+
+    def kernel(places_ref, *refs):
+        row_refs, refs = refs[: len(rows)], refs[len(rows) :]
+        third_refs, refs = refs[:planes], refs[planes:]
+        sum_refs, outs = refs[:PLANE], refs[PLANE + len(kept) :]
+        me = lax.axis_index("wide")
+        core, plane = lax.rem(me, 2), lax.div(me, PLANE)
+        total = jnp.zeros((PLANE * BLK, ranks), jnp.float32)
+        for d in range(planes):
+            for half in range(2):
+                piece = half * planes + (plane ^ d)
+                parts = [row_refs[0][core ^ k, piece] for k in range(2)]
+                parts += [ref[piece] for ref in row_refs[1:]]
+                total += jnp.dot(
+                    jnp.concatenate(parts, axis=0),
+                    third_refs[d][slots[d], half, pl.ds(0, run)],
+                    preferred_element_type=jnp.float32,
+                )
+        for k in range(PLANE):
+            anew = places_ref[k, pl.ds(0, 1)] == USUAL
+            news = [(0, total[k * BLK : (k + 1) * BLK])]
+            for d in range(planes):
+                for half in range(2):
+                    start = BLK + (2 * d + half) * up_run
+                    news.append((start, third_refs[d][slots[d], half, pl.ds(run, up_run)]))
+            for start, new in news:
+                at = pl.ds(start, new.shape[0])
+                old = sum_refs[k][at].astype(jnp.float32)
+                outs[k][at] = jnp.where(anew, new.astype(jnp.float32), old).astype(outs[k].dtype)
+
+    return pl.pallas_call(
+        kernel,
+        out_shape=[jax.ShapeDtypeStruct(value.shape, value.dtype) for value in sums],
+        in_specs=[vmem] * (1 + len(rows) + planes + PLANE)
+        + [pl.BlockSpec(memory_space=pl.ANY)] * len(kept),
+        out_specs=[vmem] * PLANE,
+        compiler_params=pltpu.CompilerParams(vmem_limit_bytes=10 * 2**20),
+        name="amend",
+    )(places, *rows, *thirds, *sums, *kept)
 
 
 def expand(planes, up_run, sums):
@@ -456,20 +498,21 @@
         sums = [sums[0]] + [swap(sums[k], k) for k in range(1, PLANE)]
         return tuple(expand(planes, up_run, sums))
 
-    def usual(places, spread, factors, rows, held, kept):
+    def sums_of(spread, factors, rows, held):
         args = (early, (1, 3), spread, rows, factors)
         sums = shrink(planes, USUAL, run, blocks[1:], blocks[2:], *args, held[1:], whole)
-        return finish([*shrink(planes, USUAL, run, blocks[:1], (), *args, held[:1], whole), *sums])
-
-    def more(places, spread, factors, rows, held, kept):
-        third = [swap(factors[d ^ 1][:1], PLANE) for d in whole[2:]]
-        factors = factors[:2] + [jnp.concatenate([factors[d], third[d - 2]]) for d in whole[2:]]
-        sums = shrink(
-            planes, SLOTS, run, blocks, blocks, whole, (), places, rows, factors, (), whole, kept=kept
-        )
-        return finish(sums)
-
-    return lax.switch(many[0], [usual, more], places, spread, factors, rows, held, sends)
+        return [*shrink(planes, USUAL, run, blocks[:1], (), *args, held[:1], whole), *sums]
+
+    def usual(spread, factors, rows, held, kept):
+        return finish(sums_of(spread, factors, rows, held))
+
+    def more(spread, factors, rows, held, kept):
+        thirds = factors[:2] + [swap(factors[d ^ 1][:1], PLANE) for d in whole[2:]]
+        slots = [USUAL if d < 2 else 0 for d in whole]
+        sums = sums_of(spread, factors, rows, held)
+        return finish(amend(planes, run, spread, rows, thirds, slots, sums, kept))
+
+    return lax.switch(many[0], [usual, more], spread, factors, rows, held, sends)
 
 
 def solution(mesh):

time: 50.8 us -> 40.7 us (0.80)
  the two profiles are of different devices: /device:TPU:21 before, /device:TPU:0 now
where the time goes in v1:
time: 40.7 us; the launch traced here: 40.4 us
  waiting for transfers between devices  17.4 us (43%)
  starting transfers between devices  9.6 us (24%)
  Pallas kernels  7.46 us (18%)
  blocking collectives  4.58 us (11%)
  between operations  1.32 us (3%)
    ppermute x8, waiting for transfers between devices, swap(): return lax.ppermute(value, 'wide', [(i, i ^ step) for i in range(count)])  17.4 us
    ppermute x8, starting transfers between devices, swap(): return lax.ppermute(value, 'wide', [(i, i ^ step) for i in range(count)])  9.6 us
    all_to_all x1, blocking collectives, swap_cores(): lax.all_to_all(value, 'wide', 0, 0, axis_index_groups=pairs, tiled=True)  4.58 us
    pallas_call x1, Pallas kernels, choose(): pl.pallas_call(lambda *refs: choose_kernel(planes, *refs), out_shape=[jax...  2.33 us
    pallas_call x1, Pallas kernels, gather(): pl.pallas_call(lambda *refs: gather_kernel(planes, *refs), out_shape=[jax...  2.12 us
    pallas_call x3, Pallas kernels, shrink(): pl.pallas_call(kernel, out_shape=[jax.ShapeDtypeStruct((height, ranks), j...  1.9 us
    pallas_call x1, Pallas kernels, expand(): pl.pallas_call(kernel, out_shape=[jax.ShapeDtypeStruct((BLK, columns), jn...  1.11 us
  transfers between devices with their start and end apart: 8, of which 5 were waited for; matrix products, arithmetic and copies ran while one was open for 0% of the time, Pallas kernels for 9%

profile of v1, /device:TPU:0, one launch (start us, length us, event | category | flops | bytes accessed | tf_op | source)
XLA Modules:
  0.0 40.4 jit_solution(11969050421420138304)
XLA Ops:
  0.6 2.3 %choose.1 = (s32[8]{0:T(128)}, bf16[3,2,288,128]{3,2,1,0:T(8,128)(2,1)S(1)}, bf16[2,2,288,128]{3,2,1,0:T(8,128)(2,1)S(1)}, bf16[2,2,288,128]{3,2,1,0:T(8,128)(2,...) custom-call(s32[16]{0:T(128)} %refs_0_.1, s32[4]{0:T(128)} %refs_1_.2, s32[4]{0:T(128)} %refs_2_.2, ...), custom_call_target="tpu_custom_call" | custom-call | tf_op jit(solution)/shard_map/choose/pallas_call | solution.py:198
  3.0 4.0 %collective-permute-start.8 = (bf16[2,2,288,128]{3,2,1,0:T(8,128)(2,1)S(1)}, bf16[2,2,288,128]{3,2,1,0:T(8,128)(2,1)S(1)}, u32[]{:S(2)}, u32[]{:S(2)}) collective-permute-start(bf16[2,2,288,128]{3,2,1,0:T(8,128)(2,1)S(1)} %get-tuple-element.105), channel_id=1, source_target_pairs={{0,8},{1,9},{2,10},{3,11},{4,12},{5,13},{6,14},{7,15},{8,0},{9,1},... | collective-permute-start | bytes 884744 | tf_op jit(solution)/shard_map/ppermute | solution.py:88
  7.0 1.5 %collective-permute-start.9 = (bf16[8,128,256]{2,1,0:T(8,128)(2,1)S(1)}, bf16[8,128,256]{2,1,0:T(8,128)(2,1)S(1)}, u32[]{:S(2)}, u32[]{:S(2)}) collective-permute-start(bf16[8,128,256]{2,1,0:T(8,128)(2,1)S(1)} %get-tuple-element.108), channel_id=1, source_target_pairs={{0,2},{1,3},{2,0},{3,1},{4,6},{5,7},{6,4},{7,5},{8,10},{9,11},{10,... | collective-permute-start | bytes 1572872 | tf_op jit(solution)/shard_map/ppermute | solution.py:88
  8.5 0.0 collective-permute-start.10
  8.5 1.7 %collective-permute-start.11 = (bf16[3,2,288,128]{3,2,1,0:T(8,128)(2,1)S(1)}, bf16[3,2,288,128]{3,2,1,0:T(8,128)(2,1)S(1)}, u32[]{:S(2)}, u32[]{:S(2)}) collective-permute-start(bf16[3,2,288,128]{3,2,1,0:T(8,128)(2,1)S(1)} %get-tuple-element.110), channel_id=1, source_target_pairs={{0,4},{1,5},{2,6},{3,7},{4,0},{5,1},{6,2},{7,3},{8,12},{9,13},{10,... | collective-permute-start | bytes 1327112 | tf_op jit(solution)/shard_map/ppermute | solution.py:88
  10.2 0.1 collective-permute-start.12
  10.4 2.1 %gather.1 = (bf16[3,2,288,128]{3,2,1,0:T(8,128)(2,1)S(1)}, bf16[2,8,128,256]{3,2,1,0:T(8,128)(2,1)S(1)}) custom-call(s32[8]{0:T(128)} %get-tuple-element.102.refs_0_.places_ref, bf16[128,8192]{1,0:T(8,128)(2,1)} %refs_1_.3, bf16[16,2,256,128]{3,2,1,0:T(8,128)(2,1)} %refs_2_.3, bf16[16,2,32,128]{3,2,1,0:T(8,128)(2,1)} %refs_3_.3), custom_call_target="tpu_custom_call" | custom-call | tf_op jit(solution)/shard_map/gather/pallas_call | solution.py:240
  12.5 0.0 copy-start
  12.5 4.6 %all_to_all.5.refs_0_ = bf16[2,8,128,256]{3,2,1,0:T(8,128)(2,1)S(1)} all-to-all(bf16[2,8,128,256]{3,2,1,0:T(8,128)(2,1)S(1)} %get-tuple-element.103), channel_id=1, replica_groups={{0,1},{2,3},{4,5},{6,7},{8,9},{10,11},{12,13},{14,15},{16,17},{18,19},{..., dimensions={0} | all-to-all | bytes 2097152 | tf_op jit(solution)/shard_map/all_to_all | solution.py:94
  17.1 4.1 %collective-permute-done.8.refs_2_ = bf16[2,2,288,128]{3,2,1,0:T(8,128)(2,1)S(1)} collective-permute-done((bf16[2,2,288,128]{3,2,1,0:T(8,128)(2,1)S(1)}, bf16[2,2,288,128]{3,2,1,0:T(8,128)(2,1)S(1)}, u32[]{:S(2)}, u32[]{:S(2)}) %collective-permute-start.8) | collective-permute-done | bytes 294944 | tf_op jit(solution)/shard_map/ppermute | solution.py:88
  21.2 0.0 copy-done
  21.2 1.2 %shrink.9 = (f32[128,128]{1,0:T(8,128)S(1)}, f32[128,128]{1,0:T(8,128)S(1)}, s32[4,8,128]{2,1,0:T(8,128)S(1)}, s32[1]{0:T(128)}) custom-call(s32[8]{0:T(128)S(1)} %copy-done, bf16[2,8,128,256]{3,2,1,0:T(8,128)(2,1)S(1)} %all_to_all.5.refs_0_, bf16[3,2,288,128]{3,2,1,0:T(8,128)(2,1)S(1)} %get-tuple-element.104.refs_1_, ...), custom_call_target="tpu_custom_call" | custom-call | flops 3000000000 | tf_op jit(solution)/shard_map/shrink/pallas_call | solution.py:348
  23.0 8.1 %collective-permute-done.12 = bf16[2,2,288,128]{3,2,1,0:T(8,128)(2,1)S(1)} collective-permute-done((bf16[2,2,288,128]{3,2,1,0:T(8,128)(2,1)S(1)}, bf16[2,2,288,128]{3,2,1,0:T(8,128)(2,1)S(1)}, u32[]{:S(2)}, u32[]{:S(2)}) %collective-permute-start.12) | collective-permute-done | bytes 294944 | tf_op jit(solution)/shard_map/ppermute | solution.py:88
  31.2 1.4 %collective-permute-done.11 = bf16[3,2,288,128]{3,2,1,0:T(8,128)(2,1)S(1)} collective-permute-done((bf16[3,2,288,128]{3,2,1,0:T(8,128)(2,1)S(1)}, bf16[3,2,288,128]{3,2,1,0:T(8,128)(2,1)S(1)}, u32[]{:S(2)}, u32[]{:S(2)}) %collective-permute-start.11) | collective-permute-done | bytes 442400 | tf_op jit(solution)/shard_map/ppermute | solution.py:88
  32.6 0.0 collective-permute-done.9
  32.6 0.0 collective-permute-done.10
  32.6 7.8 %conditional.1 = ((bf16[128,1024]{1,0:T(8,128)(2,1)}, bf16[128,1024]{1,0:T(8,128)(2,1)})) conditional(s32[]{:T(128)} %bitcast, (s32[4,8,128]{2,1,0:T(8,128)S(1)}, bf16[2,8,128,256]{3,2,1,0:T(8,128)(2,1)S(1)}, bf16[8,128,256]{2,1,0:T(8,128)(2,1)S(1)}, bf16[8,128,256]{2,1,0:T(8,128)(2,1)S(1)}, bf16[3,2,288,128]{3,2,1,0:T(8,128)(2,1)S(1)}, ...), branch_computations={%region_0.0_spmd, %region_1.0_spmd} | conditional | bytes 2949328 | solution.py:515
  32.6 0.5 %shrink.5 = (bf16[384,128]{1,0:T(8,128)(2,1)S(1)}, bf16[384,128]{1,0:T(8,128)(2,1)S(1)}, bf16[384,128]{1,0:T(8,128)(2,1)S(1)}) custom-call(s32[4,8,128]{2,1,0:T(8,128)S(1)} %get-tuple-element.52.places_ref, bf16[2,8,128,256]{3,2,1,0:T(8,128)(2,1)S(1)} %get-tuple-element.53.refs_0_, bf16[8,128,256]{2,1,0:T(8,128)(2,1)S(1)} %get-tuple-element.54.refs_1_, ...), custom_call_target="tpu_custom_call" | custom-call | tf_op jit(solution)/shard_map/cond/branch_0_fun/shrink/pallas_call | solution.py:348
  33.1 1.1 %collective-permute-start = (bf16[384,128]{1,0:T(8,128)(2,1)S(1)}, bf16[384,128]{1,0:T(8,128)(2,1)S(1)}, u32[]{:S(2)}, u32[]{:S(2)}) collective-permute-start(bf16[384,128]{1,0:T(8,128)(2,1)S(1)} %get-tuple-element.61), channel_id=1, source_target_pairs={{0,2},{1,3},{2,0},{3,1},{4,6},{5,7},{6,4},{7,5},{8,10},{9,11},{10,... | collective-permute-start | bytes 294920 | tf_op jit(solution)/shard_map/cond/branch_0_fun/ppermute | solution.py:88
  34.3 0.1 collective-permute-start.1
  34.3 1.0 %collective-permute-start.2 = (bf16[384,128]{1,0:T(8,128)(2,1)S(1)}, bf16[384,128]{1,0:T(8,128)(2,1)S(1)}, u32[]{:S(2)}, u32[]{:S(2)}) collective-permute-start(bf16[384,128]{1,0:T(8,128)(2,1)S(1)} %get-tuple-element.63), channel_id=1, source_target_pairs={{0,1},{1,0},{2,3},{3,2},{4,5},{5,4},{6,7},{7,6},{8,9},{9,8},{10,11... | collective-permute-start | bytes 294920 | tf_op jit(solution)/shard_map/cond/branch_0_fun/ppermute | solution.py:88
  35.3 0.2 shrink.6.refs_3_
  35.6 2.9 %collective-permute-done.refs_0_ = bf16[384,128]{1,0:T(8,128)(2,1)S(1)} collective-permute-done((bf16[384,128]{1,0:T(8,128)(2,1)S(1)}, bf16[384,128]{1,0:T(8,128)(2,1)S(1)}, u32[]{:S(2)}, u32[]{:S(2)}) %collective-permute-start) | collective-permute-done | bytes 98336 | tf_op jit(solution)/shard_map/cond/branch_0_fun/ppermute | solution.py:88
  38.4 0.8 %collective-permute-done.1.refs_1_ = bf16[384,128]{1,0:T(8,128)(2,1)S(1)} collective-permute-done((bf16[384,128]{1,0:T(8,128)(2,1)S(1)}, bf16[384,128]{1,0:T(8,128)(2,1)S(1)}, u32[]{:S(2)}, u32[]{:S(2)}) %collective-permute-start.1) | collective-permute-done | bytes 98336 | tf_op jit(solution)/shard_map/cond/branch_0_fun/ppermute | solution.py:88
  39.3 0.0 collective-permute-done.2.refs_2_
  39.3 1.1 %expand.2 = (bf16[128,1024]{1,0:T(8,128)(2,1)}, bf16[128,1024]{1,0:T(8,128)(2,1)}) custom-call(bf16[384,128]{1,0:T(8,128)(2,1)S(1)} %collective-permute-done.refs_0_, bf16[384,128]{1,0:T(8,128)(2,1)S(1)} %collective-permute-done.1.refs_1_, bf16[384,128]{1,0:T(8,128)(2,1)S(1)} %collective-permute-done.2.refs_2_, f32[384,128]{1,0:T(8,128)S(1)} %shrink.6.refs_3_), custom_call_target="tpu_custom_call" | custom-call | tf_op jit(solution)/shard_map/cond/branch_0_fun/expand/pallas_call | solution.py:445
Async XLA Ops:
  3.0 18.2 %collective-permute-start.8 = (bf16[2,2,288,128]{3,2,1,0:T(8,128)(2,1)S(1)}, bf16[2,2,288,128]{3,2,1,0:T(8,128)(2,1)S(1)}, u32[]{:S(2)}, u32[]{:S(2)}) collective-permute-start(bf16[2,2,288,128]{3,2,1,0:T(8,128)(2,1)S(1)} %get-tuple-element.105), channel_id=1, source_target_pairs={{0,8},{1,9},{2,10},{3,11},{4,12},{5,13},{6,14},{7,15},{8,0},{9,1},... | collective-permute-start | bytes 884744 | tf_op jit(solution)/shard_map/ppermute | solution.py:88
  7.0 25.6 %collective-permute-start.9 = (bf16[8,128,256]{2,1,0:T(8,128)(2,1)S(1)}, bf16[8,128,256]{2,1,0:T(8,128)(2,1)S(1)}, u32[]{:S(2)}, u32[]{:S(2)}) collective-permute-start(bf16[8,128,256]{2,1,0:T(8,128)(2,1)S(1)} %get-tuple-element.108), channel_id=1, source_target_pairs={{0,2},{1,3},{2,0},{3,1},{4,6},{5,7},{6,4},{7,5},{8,10},{9,11},{10,... | collective-permute-start | bytes 1572872 | tf_op jit(solution)/shard_map/ppermute | solution.py:88
  8.5 24.1 %collective-permute-start.10 = (bf16[8,128,256]{2,1,0:T(8,128)(2,1)S(1)}, bf16[8,128,256]{2,1,0:T(8,128)(2,1)S(1)}, u32[]{:S(2)}, u32[]{:S(2)}) collective-permute-start(bf16[8,128,256]{2,1,0:T(8,128)(2,1)S(1)} %get-tuple-element.109), channel_id=1, source_target_pairs={{0,3},{1,2},{2,1},{3,0},{4,7},{5,6},{6,5},{7,4},{8,11},{9,10},{10,... | collective-permute-start | bytes 1572872 | tf_op jit(solution)/shard_map/ppermute | solution.py:88
  8.5 24.1 %collective-permute-start.11 = (bf16[3,2,288,128]{3,2,1,0:T(8,128)(2,1)S(1)}, bf16[3,2,288,128]{3,2,1,0:T(8,128)(2,1)S(1)}, u32[]{:S(2)}, u32[]{:S(2)}) collective-permute-start(bf16[3,2,288,128]{3,2,1,0:T(8,128)(2,1)S(1)} %get-tuple-element.110), channel_id=1, source_target_pairs={{0,4},{1,5},{2,6},{3,7},{4,0},{5,1},{6,2},{7,3},{8,12},{9,13},{10,... | collective-permute-start | bytes 1327112 | tf_op jit(solution)/shard_map/ppermute | solution.py:88
  10.2 21.0 %collective-permute-start.12 = (bf16[2,2,288,128]{3,2,1,0:T(8,128)(2,1)S(1)}, bf16[2,2,288,128]{3,2,1,0:T(8,128)(2,1)S(1)}, u32[]{:S(2)}, u32[]{:S(2)}) collective-permute-start(bf16[2,2,288,128]{3,2,1,0:T(8,128)(2,1)S(1)} %get-tuple-element.111), channel_id=1, source_target_pairs={{0,12},{1,13},{2,14},{3,15},{4,8},{5,9},{6,10},{7,11},{8,4},{9,5},... | collective-permute-start | bytes 884744 | tf_op jit(solution)/shard_map/ppermute | solution.py:88
  12.5 8.7 %copy-start = (s32[8]{0:T(128)S(1)}, s32[8]{0:T(128)}, u32[]{:S(2)}) copy-start(s32[8]{0:T(128)} %get-tuple-element.102.refs_0_.places_ref) | copy-start | bytes 100
  33.1 5.3 %collective-permute-start = (bf16[384,128]{1,0:T(8,128)(2,1)S(1)}, bf16[384,128]{1,0:T(8,128)(2,1)S(1)}, u32[]{:S(2)}, u32[]{:S(2)}) collective-permute-start(bf16[384,128]{1,0:T(8,128)(2,1)S(1)} %get-tuple-element.61), channel_id=1, source_target_pairs={{0,2},{1,3},{2,0},{3,1},{4,6},{5,7},{6,4},{7,5},{8,10},{9,11},{10,... | collective-permute-start | bytes 294920 | tf_op jit(solution)/shard_map/cond/branch_0_fun/ppermute | solution.py:88
  34.3 5.0 %collective-permute-start.1 = (bf16[384,128]{1,0:T(8,128)(2,1)S(1)}, bf16[384,128]{1,0:T(8,128)(2,1)S(1)}, u32[]{:S(2)}, u32[]{:S(2)}) collective-permute-start(bf16[384,128]{1,0:T(8,128)(2,1)S(1)} %get-tuple-element.62), channel_id=1, source_target_pairs={{0,3},{1,2},{2,1},{3,0},{4,7},{5,6},{6,5},{7,4},{8,11},{9,10},{10,... | collective-permute-start | bytes 294920 | tf_op jit(solution)/shard_map/cond/branch_0_fun/ppermute | solution.py:88
  34.3 5.0 %collective-permute-start.2 = (bf16[384,128]{1,0:T(8,128)(2,1)S(1)}, bf16[384,128]{1,0:T(8,128)(2,1)S(1)}, u32[]{:S(2)}, u32[]{:S(2)}) collective-permute-start(bf16[384,128]{1,0:T(8,128)(2,1)S(1)} %get-tuple-element.63), channel_id=1, source_target_pairs={{0,1},{1,0},{2,3},{3,2},{4,5},{5,4},{6,7},{7,6},{8,9},{9,8},{10,11... | collective-permute-start | bytes 294920 | tf_op jit(solution)/shard_map/cond/branch_0_fun/ppermute | solution.py:88
